TPU v7x, 32 devices: a whole 2x2x4 slice. The times are simulated.
32 devices in a mesh: dp: 2 (over x), fsdp: 16 (over z, y, core).
Axes of the slice: x: 2, y: 2, z: 4, core: 2. Of those that a mesh axis runs over, the one named last changes fastest.
Arguments:
- hidden: bfloat16 [64, 64, 768], P(('dp', 'fsdp')), may hold values from -6 to 6
- lengths: int32 [64], P(('dp', 'fsdp')), may hold values from 5 to 32, as said below
- features: bfloat16 [64, 257, 1408], P(('dp', 'fsdp')), may hold values from -6 to 6
- cotangent: bfloat16 [64, 64, 768], P(('dp', 'fsdp')), may hold values from -6 to 6
- self_params: bfloat16 [2363392], P('fsdp')
- cross_params: bfloat16 [3346432], P('fsdp')
- ffn_params: bfloat16 [9449472], P('fsdp')
Outputs:
- mixed: bfloat16 [64, 64, 768], P(('dp', 'fsdp'))
- hidden_grad: bfloat16 [64, 64, 768], P(('dp', 'fsdp'))
- self_grad: float32 [2363392], P('fsdp')
- cross_grad: float32 [3346432], P('fsdp')
- ffn_grad: float32 [9449472], P('fsdp')
Inputs may be any that keep to these rules, and one draw needn't show every extreme that they name: lengths lie between 5 and 32; some item of every draw has 32.
All inputs are finite; a program needn't handle non-finite values.
Results may differ from a plain program's by a relative error of at most 0.017.
Values may be sent and summed in bfloat16 or wider, within the bound.
A program may use at most 384 MiB of HBM per device.

v0:
```python
from functools import partial
import math
import jax
import jax.numpy as jnp
from jax import lax
from jax.sharding import PartitionSpec as P

D = 768
HEADS = 12
HDIM = 64
F = 3072
E = 1408
NQ = 32
EPS = 1e-06
SCALE = 0.125


def self_layout():
    return [(D, D)] * 4 + [(D,)] * 5


def cross_layout():
    return [(D, D), (E, D), (E, D), (D, D)] + [(D,)] * 5


def ffn_layout():
    return [(D, F), (F,), (F, D), (D,), (D,), (D,)] * 2


def split_flat(flat_vec, layouts):
    pieces = []
    offset = 0
    for layout in layouts:
        amount = math.prod(layout)
        pieces.append(flat_vec[offset : offset + amount].reshape(layout))
        offset = offset + amount
    return pieces


def join_flat(pieces, length):
    flat_vec = jnp.concatenate([piece.reshape(-1) for piece in pieces])
    return jnp.pad(flat_vec, (0, length - flat_vec.shape[0]))


def regroup(flat_vec):
    groups = lax.axis_size("fsdp")
    replicas = lax.axis_size("dp")
    return flat_vec.reshape(groups, replicas, -1).transpose(1, 0, 2).reshape(-1)


def matmul(left, right):
    return jnp.dot(left, right, preferred_element_type=jnp.float32)


def matmul_left(left, right):
    return lax.dot_general(
        left, right, (((0,), (0,)), ((), ())), preferred_element_type=jnp.float32
    )


def matmul_right(left, right):
    return lax.dot_general(
        left, right, (((1,), (1,)), ((), ())), preferred_element_type=jnp.float32
    )


def column_sum(values):
    return jnp.sum(values.astype(jnp.float32), 0)


def layer_norm(values, gain, shift):
    average = jnp.mean(values, -1, keepdims=True)
    centered = values - average
    variance = jnp.mean(centered * centered, -1, keepdims=True)
    return centered * lax.rsqrt(variance + EPS) * gain + shift


def norm_backward(summed, gain, shift, grad_out):
    _, norm_pull = jax.vjp(layer_norm, summed, gain.astype(jnp.float32), shift.astype(jnp.float32))
    return norm_pull(grad_out)


def heads(rows, items):
    return rows.reshape(items, -1, HEADS, HDIM)


def score_block(query, keys, mask):
    scores = jnp.einsum("iqhd,ikhd->ihqk", query, keys, preferred_element_type=jnp.float32) * SCALE
    if mask is not None:
        scores = jnp.where(mask, scores, -1e30)
    return scores


def attend(query, keys, values, mask):
    scores = score_block(query, keys, mask)
    top_sum = jax.nn.logsumexp(scores, axis=-1)
    probs = jnp.exp(scores - top_sum[..., None]).astype(jnp.bfloat16)
    context = jnp.einsum("ihqk,ikhd->iqhd", probs, values, preferred_element_type=jnp.float32)
    return (context, top_sum)


def attend_back(query, keys, values, mask, top_sum, grad_context):
    probs = jnp.exp(score_block(query, keys, mask) - top_sum[..., None])
    grad_probs = jnp.einsum(
        "iqhd,ikhd->ihqk", grad_context, values, preferred_element_type=jnp.float32
    )
    inner = jnp.sum(probs * grad_probs, -1, keepdims=True)
    grad_scores = (probs * (grad_probs - inner)).astype(jnp.bfloat16)
    grad_query = (
        jnp.einsum("ihqk,ikhd->iqhd", grad_scores, keys, preferred_element_type=jnp.float32) * SCALE
    )
    grad_keys = (
        jnp.einsum("ihqk,iqhd->ikhd", grad_scores, query, preferred_element_type=jnp.float32)
        * SCALE
    )
    grad_values = jnp.einsum(
        "ihqk,iqhd->ikhd",
        probs.astype(jnp.bfloat16),
        grad_context,
        preferred_element_type=jnp.float32,
    )
    return (grad_query, grad_keys, grad_values)


def linear_back(inputs, weight, grad_out):
    return (matmul_left(inputs, grad_out), column_sum(grad_out), matmul_right(grad_out, weight))


def ffn_forward(rows, params):
    w_in, b_in, w_out, b_out, gain, shift = params
    rows_low = rows.astype(jnp.bfloat16)
    hidden_pre = matmul(rows_low, w_in) + b_in
    activated = jax.nn.gelu(hidden_pre, approximate=True).astype(jnp.bfloat16)
    summed = rows + (matmul(activated, w_out) + b_out)
    final = layer_norm(summed, gain.astype(jnp.float32), shift.astype(jnp.float32))
    return (final, (rows_low, hidden_pre, activated, summed))


def ffn_backward(grad_out, kept, params):
    w_in, b_in, w_out, b_out, gain, shift = params
    rows_low, hidden_pre, activated, summed = kept
    grad_sum, grad_gain, grad_shift = norm_backward(summed, gain, shift, grad_out)
    grad_branch = grad_sum.astype(jnp.bfloat16)
    grad_w_out, grad_b_out, grad_act = linear_back(activated, w_out, grad_branch)
    _, gelu_pull = jax.vjp(partial(jax.nn.gelu, approximate=True), hidden_pre)
    grad_pre = gelu_pull(grad_act)[0].astype(jnp.bfloat16)
    grad_w_in, grad_b_in, grad_rows = linear_back(rows_low, w_in, grad_pre)
    return (
        grad_sum + grad_rows,
        [grad_w_in, grad_b_in, grad_w_out, grad_b_out, grad_gain, grad_shift],
    )


def per_device(hidden, lengths, features, cotangent, self_params, cross_params, ffn_params):
    items, seq, width = hidden.shape
    self_full = lax.all_gather(self_params, "fsdp", axis=0, tiled=True)
    self_parts = split_flat(self_full, self_layout())
    w_q, w_k, w_v, w_o, b_q, b_v, b_o, gain_one, shift_one = self_parts
    positions = jnp.arange(seq)
    rows_at = positions[:, None]
    cols_at = positions[None, :]
    allowed = (cols_at < NQ)[None] | ((rows_at >= NQ) & (cols_at <= rows_at))[None] & (
        cols_at[None] < NQ + lengths[:, None, None]
    )
    allowed = allowed[:, None]
    inputs = hidden.reshape(-1, width)
    query_low = (matmul(inputs, w_q) + b_q).astype(jnp.bfloat16)
    key_low = matmul(inputs, w_k).astype(jnp.bfloat16)
    value_low = (matmul(inputs, w_v) + b_v).astype(jnp.bfloat16)
    context, self_top = attend(
        heads(query_low, items), heads(key_low, items), heads(value_low, items), allowed
    )
    context_low = context.reshape(-1, width).astype(jnp.bfloat16)
    summed_one = inputs.astype(jnp.float32) + (matmul(context_low, w_o) + b_o)
    first = layer_norm(summed_one, gain_one.astype(jnp.float32), shift_one.astype(jnp.float32))
    first_items = first.reshape(items, seq, width)
    query_rows = first_items[:, :NQ].reshape(-1, width)
    text_rows = first_items[:, NQ:].reshape(-1, width)
    cross_full = lax.all_gather(cross_params, "fsdp", axis=0, tiled=True)
    cross_parts = split_flat(cross_full, cross_layout())
    cross_wq, cross_wk, cross_wv, cross_wo, cross_bq, cross_bv, cross_bo, gain_two, shift_two = (
        cross_parts
    )
    query_in = query_rows.astype(jnp.bfloat16)
    image_rows = features.reshape(-1, features.shape[-1])
    cross_query = (matmul(query_in, cross_wq) + cross_bq).astype(jnp.bfloat16)
    cross_key = matmul(image_rows, cross_wk).astype(jnp.bfloat16)
    cross_value = (matmul(image_rows, cross_wv) + cross_bv).astype(jnp.bfloat16)
    cross_context, cross_top = attend(
        heads(cross_query, items), heads(cross_key, items), heads(cross_value, items), None
    )
    cross_low = cross_context.reshape(-1, width).astype(jnp.bfloat16)
    summed_two = query_rows + (matmul(cross_low, cross_wo) + cross_bo)
    second = layer_norm(summed_two, gain_two.astype(jnp.float32), shift_two.astype(jnp.float32))
    ffn_full = lax.all_gather(ffn_params, "fsdp", axis=0, tiled=True)
    ffn_parts = split_flat(ffn_full, ffn_layout())
    query_final, query_kept = ffn_forward(second, ffn_parts[:6])
    text_final, text_kept = ffn_forward(text_rows, ffn_parts[6:])
    mixed = jnp.concatenate(
        [query_final.reshape(items, NQ, width), text_final.reshape(items, -1, width)], 1
    ).astype(jnp.bfloat16)
    grad_items = cotangent.astype(jnp.float32)
    grad_query_final = grad_items[:, :NQ].reshape(-1, width)
    grad_text_final = grad_items[:, NQ:].reshape(-1, width)
    ffn_back = split_flat(lax.all_gather(ffn_params, "fsdp", axis=0, tiled=True), ffn_layout())
    grad_second, query_grads = ffn_backward(grad_query_final, query_kept, ffn_back[:6])
    grad_text, text_grads = ffn_backward(grad_text_final, text_kept, ffn_back[6:])
    ffn_flat_grad = join_flat(query_grads + text_grads, ffn_full.shape[0])
    ffn_grad = lax.psum_scatter(
        regroup(ffn_flat_grad), ("dp", "fsdp"), scatter_dimension=0, tiled=True
    )
    cross_back = split_flat(
        lax.all_gather(cross_params, "fsdp", axis=0, tiled=True), cross_layout()
    )
    grad_summed_two, grad_gain_two, grad_shift_two = norm_backward(
        summed_two, cross_back[7], cross_back[8], grad_second
    )
    grad_cross_out = grad_summed_two.astype(jnp.bfloat16)
    grad_cross_wo, grad_cross_bo, grad_cross_ctx = linear_back(
        cross_low, cross_back[3], grad_cross_out
    )
    grad_cq, grad_ck, grad_cv = attend_back(
        heads(cross_query, items),
        heads(cross_key, items),
        heads(cross_value, items),
        None,
        cross_top,
        heads(grad_cross_ctx.astype(jnp.bfloat16), items),
    )
    grad_cq = grad_cq.reshape(-1, width).astype(jnp.bfloat16)
    grad_ck = grad_ck.reshape(-1, width).astype(jnp.bfloat16)
    grad_cv = grad_cv.reshape(-1, width).astype(jnp.bfloat16)
    grad_cross_wq, grad_cross_bq, grad_query_in = linear_back(query_in, cross_back[0], grad_cq)
    grad_cross_wk = matmul_left(image_rows, grad_ck)
    grad_cross_wv = matmul_left(image_rows, grad_cv)
    grad_cross_bv = column_sum(grad_cv)
    grad_query_rows = grad_summed_two + grad_query_in
    cross_list = [
        grad_cross_wq,
        grad_cross_wk,
        grad_cross_wv,
        grad_cross_wo,
        grad_cross_bq,
        grad_cross_bv,
        grad_cross_bo,
        grad_gain_two,
        grad_shift_two,
    ]
    cross_flat_grad = join_flat(cross_list, cross_full.shape[0])
    cross_grad = lax.psum_scatter(
        regroup(cross_flat_grad), ("dp", "fsdp"), scatter_dimension=0, tiled=True
    )
    self_back = split_flat(lax.all_gather(self_params, "fsdp", axis=0, tiled=True), self_layout())
    grad_first = jnp.concatenate(
        [grad_query_rows.reshape(items, NQ, width), grad_text.reshape(items, -1, width)], 1
    ).reshape(-1, width)
    grad_summed_one, grad_gain_one, grad_shift_one = norm_backward(
        summed_one, self_back[7], self_back[8], grad_first
    )
    grad_attn = grad_summed_one.astype(jnp.bfloat16)
    grad_w_o, grad_b_o, grad_ctx = linear_back(context_low, self_back[3], grad_attn)
    grad_q, grad_k, grad_v = attend_back(
        heads(query_low, items),
        heads(key_low, items),
        heads(value_low, items),
        allowed,
        self_top,
        heads(grad_ctx.astype(jnp.bfloat16), items),
    )
    grad_q = grad_q.reshape(-1, width).astype(jnp.bfloat16)
    grad_k = grad_k.reshape(-1, width).astype(jnp.bfloat16)
    grad_v = grad_v.reshape(-1, width).astype(jnp.bfloat16)
    grad_w_q, grad_b_q, input_from_q = linear_back(inputs, self_back[0], grad_q)
    grad_w_k = matmul_left(inputs, grad_k)
    input_from_k = matmul_right(grad_k, self_back[1])
    grad_w_v, grad_b_v, input_from_v = linear_back(inputs, self_back[2], grad_v)
    hidden_grad = (
        (grad_summed_one + input_from_q + input_from_k + input_from_v)
        .reshape(items, seq, width)
        .astype(jnp.bfloat16)
    )
    self_list = [
        grad_w_q,
        grad_w_k,
        grad_w_v,
        grad_w_o,
        grad_b_q,
        grad_b_v,
        grad_b_o,
        grad_gain_one,
        grad_shift_one,
    ]
    self_flat_grad = join_flat(self_list, self_full.shape[0])
    self_grad = lax.psum_scatter(
        regroup(self_flat_grad), ("dp", "fsdp"), scatter_dimension=0, tiled=True
    )
    self_grad, cross_grad, ffn_grad = (
        lax.all_gather(self_grad.astype(jnp.bfloat16), "dp", axis=0, tiled=True).astype(
            self_grad.dtype
        ),
        lax.all_gather(cross_grad.astype(jnp.bfloat16), "dp", axis=0, tiled=True).astype(
            cross_grad.dtype
        ),
        lax.all_gather(ffn_grad.astype(jnp.bfloat16), "dp", axis=0, tiled=True).astype(
            ffn_grad.dtype
        ),
    )
    return (mixed, hidden_grad, self_grad, cross_grad, ffn_grad)


def solution(mesh):
    return jax.shard_map(
        per_device,
        mesh=mesh,
        in_specs=(
            P(("dp", "fsdp"), None, None),
            P(("dp", "fsdp")),
            P(("dp", "fsdp"), None, None),
            P(("dp", "fsdp"), None, None),
            P("fsdp"),
            P("fsdp"),
            P("fsdp"),
        ),
        out_specs=(
            P(("dp", "fsdp"), None, None),
            P(("dp", "fsdp"), None, None),
            P("fsdp"),
            P("fsdp"),
            P("fsdp"),
        ),
        check_vma=False,
    )
```

profile of v0, /device:TPU:0, one launch (start us, length us, event | category | flops | bytes accessed | tf_op | source)
XLA Modules:
  0.0 2604.6 jit_solution(10896527017699016095)
XLA Ops:
  17.5 14.2 reshape.500
  35.5 60.6 %all-gather.11.cloned.1.call-done = bf16[16,1,147712]{2,1,0:T(2,128)(2,1)} async-done(((bf16[1,1,147712]{2,1,0:T(2,128)(2,1)}), bf16[16,1,147712]{2,1,0:T(2,128)(2,1)}) %all-gather.11.cloned.1.call-update) | async-done | bytes 4726800 | tf_op jit(solution)/shard_map/all_gather | solution.py:156
  96.1 78.1 %reduce.11 = bf16[16,147712]{1,0:T(8,128)(2,1)} reduce(bf16[16,1,147712]{2,1,0:T(2,128)(2,1)} %all-gather.11.cloned.1.call-done, bf16[]{:T(256)} %constant.79), dimensions={1}, to_apply=%all-gather.reduce_sub_computation | reduce | bytes 9453570 | tf_op jit(solution)/shard_map/all_gather | solution.py:156
  174.2 10.1 reshape.497
  209.2 141.5 %reduce.12 = bf16[16,209152]{1,0:T(8,128)(2,1)} reduce(bf16[16,1,209152]{2,1,0:T(2,128)(2,1)} %all-gather.13.cloned.1.call-done, bf16[]{:T(256)} %constant.79), dimensions={1}, to_apply=%all-gather.1.reduce_sub_computation | reduce | bytes 13385730 | tf_op jit(solution)/shard_map/all_gather | solution.py:179
  350.8 14.0 reshape.499
  420.2 400.6 %reduce.13 = bf16[16,590592]{1,0:T(8,128)(2,1)} reduce(bf16[16,1,590592]{2,1,0:T(2,128)(2,1)} %all-gather.15.cloned.1.call-done, bf16[]{:T(256)} %constant.79), dimensions={1}, to_apply=%all-gather.2.reduce_sub_computation | reduce | bytes 37797888 | tf_op jit(solution)/shard_map/all_gather | solution.py:195
  820.8 43.1 %reshape.501 = bf16[9449472]{0:T(1024)(128)(2,1)} reshape(bf16[16,590592]{1,0:T(8,128)(2,1)} %reduce.13) | data formatting | bytes 37797888
  863.9 14.0 fusion.71
  1047.3 10.3 reshape.482
  1148.6 13.4 reshape.488
  1162.0 10.4 copy.156
  1192.0 10.8 reshape.491
  1210.0 10.8 reshape.493
  1233.6 80.5 %dynamic-update-slice.6 = f32[9447936]{0:T(1024)} dynamic-update-slice(f32[9447936]{0:T(1024)} %constant_dynamic-update-slice_fusion.25, f32[2359296]{0:T(1024)} %bitcast.168, s32[]{} %constant.91) | dynamic-update-slice | bytes 18874372
  1315.4 80.5 %dynamic-update-slice.8 = f32[9447936]{0:T(1024)} dynamic-update-slice(f32[9447936]{0:T(1024)} %constant_dynamic-update-slice_fusion.24, f32[2359296]{0:T(1024)} %reshape.493, s32[]{} %constant.93) | dynamic-update-slice | bytes 18874372
  1399.8 27.1 %pad.14 = f32[9449472]{0:T(1024)} pad(f32[9447936]{0:T(1024)} %constant_dynamic-update-slice_fusion.21, f32[]{:T(128)} %constant.23.clone.1), padding=0_1536 | pad | bytes 75589632 | tf_op jit(solution)/shard_map/jit(_pad)/pad | solution.py:42
  1426.9 59.6 %reshape.494 = f32[16,2,295296]{2,1,0:T(2,128)} reshape(f32[9449472]{0:T(1024)} %pad.14) | data formatting | bytes 75595776 | tf_op jit(solution)/shard_map/reshape | solution.py:48
  1486.5 29.9 %copy.157 = f32[2,16,295296]{2,1,0:T(8,128)} copy(f32[2,16,295296]{2,0,1:T(2,128)} %bitcast.161) | data formatting | bytes 75595776 | tf_op jit(solution)/shard_map/transpose | solution.py:48
  1516.4 31.6 %reshape.495 = f32[9449472]{0:T(1024)} reshape(f32[2,16,295296]{2,1,0:T(8,128)} %copy.157) | data formatting | bytes 75595776 | tf_op jit(solution)/shard_map/reshape | solution.py:48
  1548.0 960.9 %all-reduce.8 = (bf16[2363392]{0:T(1024)(128)(2,1)}, bf16[3346432]{0:T(1024)(128)(2,1)}, bf16[9449472]{0:T(1024)(128)(2,1)}) all-reduce(f32[2363392]{0:T(1024)} %reshape.483, f32[3346432]{0:T(1024)} %reshape.489, f32[9449472]{0:T(1024)} %reshape.495), channel_id=2, replica_groups=mesh['dp'=2,'fsdp'=16] {'dp','fsdp'}, use_global_device_ids=true, to_apply=%region_28.29.clone | all-reduce | flops 15159296 | bytes 90955776
  2531.3 14.9 all-gather.4
  2557.1 10.7 all-gather.17.cloned.1.call-done
  2567.8 26.9 %convert_reduce_fusion = f32[2,295296]{1,0:T(2,128)S(1)} fusion(bf16[2,1,295296]{2,1,0:T(2,128)(2,1)} %all-gather.17.cloned.1.call-done), kind=kLoop, calls=%fused_computation.6 | loop fusion | flops 590592 | bytes 3543552 | tf_op jit(solution)/shard_map/convert_element_type | solution.py:304
  (496 shorter events, 434.8 us)
Async XLA Ops:
  7.2 10.3 copy-start.56
  7.2 88.9 %all-gather.11.cloned.1.call-start = ((), (), s32[]{:S(2)}) async-start(), calls=%async_computation | async-start | bytes 10044416 | tf_op jit(solution)/shard_map/all_gather | solution.py:156
  11.7 197.5 %all-gather.13.cloned.1.call-start = ((), (), s32[]{:S(2)}) async-start(), calls=%async_computation.1 | async-start | bytes 14222336 | tf_op jit(solution)/shard_map/all_gather | solution.py:179
  17.4 14.4 copy-start.34
  17.4 402.8 %all-gather.15.cloned.1.call-start = ((), (), s32[]{:S(2)}) async-start(), calls=%async_computation.2 | async-start | bytes 40160256 | tf_op jit(solution)/shard_map/all_gather | solution.py:195
  31.7 2536.1 %all-gather.17.cloned.1.call-start = ((), (), s32[]{:S(2)}) async-start(), calls=%async_computation.3 | async-start | bytes 3543552 | tf_op jit(solution)/shard_map/all_gather | solution.py:304
  204.9 145.9 %copy-start.7 = (bf16[768,768]{1,0:T(8,128)(2,1)}, bf16[768,768]{1,0:T(8,128)(2,1)S(1)}, u32[]{:S(2)}) copy-start(bf16[768,768]{1,0:T(8,128)(2,1)S(1)} %reshape.456) | copy-start | bytes 3538948
  207.8 143.0 %copy-start.44 = (f32[2,32,768]{2,1,0:T(8,128)}, f32[2,32,768]{2,1,0:T(8,128)S(1)}, u32[]{:S(2)}) copy-start(f32[2,32,768]{2,1,0:T(8,128)S(1)} %get-tuple-element.72) | copy-start | bytes 589828
  208.6 196.8 %copy-start.59 = (bf16[2,32,768]{2,1,0:T(8,128)(2,1)}, bf16[2,32,768]{2,1,0:T(8,128)(2,1)S(1)}, u32[]{:S(2)}) copy-start(bf16[2,32,768]{2,1,0:T(8,128)(2,1)S(1)} %get-tuple-element.69) | copy-start | bytes 294916
  898.2 12.2 slice-start.2
  901.8 8.5 slice-start.3
  992.6 12.9 copy-start.40
  994.2 19.5 copy-start.46
  1192.0 10.8 copy-start.51
  1192.0 10.8 copy-start.64
  1210.0 10.8 copy-start.113
  1221.4 9.6 copy-start.102
  1221.4 11.0 copy-start.101
  1233.6 80.5 %copy-start.114 = (f32[3072]{0:T(1024)S(1)}, f32[3072]{0:T(1024)}, u32[]{:S(2)}) copy-start(f32[3072]{0:T(1024)} %get-tuple-element.21) | copy-start | bytes 36868
  1315.4 80.5 %copy-start.105 = (f32[768]{0:T(1024)S(1)}, f32[768]{0:T(1024)}, u32[]{:S(2)}) copy-start(f32[768]{0:T(1024)} %get-tuple-element.19) | copy-start | bytes 9220
  1315.4 81.8 %copy-start.104 = (f32[768]{0:T(1024)S(1)}, f32[768]{0:T(1024)}, u32[]{:S(2)}) copy-start(f32[768]{0:T(1024)} %get-tuple-element.7) | copy-start | bytes 9220
  1315.4 83.1 %copy-start.100 = (f32[768]{0:T(1024)S(1)}, f32[768]{0:T(1024)}, u32[]{:S(2)}) copy-start(f32[768]{0:T(1024)} %get-tuple-element.13) | copy-start | bytes 9220
  2546.2 8.5 copy-start.39
  2546.2 8.5 copy-start.122
  (115 other events, 385.5 us)
Sparse Core Ops, SparseCore 0:
  11.8 84.2 all-gather.10
  98.9 103.9 all-gather.12
  205.1 186.1 all-gather.14
  2531.4 36.2 all-gather.16
where the time goes:
time: 2630 us; the launch traced here: 2600 us
  blocking collectives  984 us (37%)
  local copies, waits for them, and re-layouts  767 us (29%)
  other arithmetic  672 us (26%)
  matrix products  94.1 us (4%)
  waiting for transfers between devices  71.3 us (3%)
    unnamed x1, blocking collectives  961 us
    all_gather x1, other arithmetic, per_device(): ffn_full = lax.all_gather(ffn_params, 'fsdp', axis=0, tiled=True)  401 us
    unnamed x312, local copies, waits for them, and re-layouts  337 us
    all_gather x1, other arithmetic, per_device(): cross_full = lax.all_gather(cross_params, 'fsdp', axis=0, tiled=True)  142 us
    reshape x6, local copies, waits for them, and re-layouts, regroup(): return flat_vec.reshape(groups, replicas, -1).transpose(1, 0, 2).reshape(-1)  133 us
    all_gather x1, other arithmetic, per_device(): self_full = lax.all_gather(self_params, 'fsdp', axis=0, tiled=True)  78.1 us
    all_gather x1, waiting for transfers between devices, per_device(): self_full = lax.all_gather(self_params, 'fsdp', axis=0, tiled=True)  60.6 us
  transfers between devices with their start and end apart: 4, of which 2 were waited for; matrix products, arithmetic and copies ran while one was open for 14% of the time, Pallas kernels for 0%

commit v1 on v0

--- a/solution.py
+++ b/solution.py
@@ -153,7 +153,40 @@
 
 def per_device(hidden, lengths, features, cotangent, self_params, cross_params, ffn_params):
     items, seq, width = hidden.shape
-    self_full = lax.all_gather(self_params, "fsdp", axis=0, tiled=True)
+
+    def sides_process(frame, axis_key, ndim_at):
+        o_now, part_now, finding = (
+            lax.psum(1, axis_key),
+            lax.axis_index(axis_key),
+            frame.shape[ndim_at],
+        )
+        sheets = []
+        for rr, dd in enumerate(frame.shape):
+            sheets.append(dd * o_now if rr == ndim_at else dd)
+        x_next = jnp.zeros(sheets, frame.dtype)
+        current_arr = lax.dynamic_update_slice_in_dim(
+            x_next, frame, part_now * finding, axis=ndim_at
+        )
+        w1 = response = frame
+        for ix in range(1, o_now // 2 + 1):
+            steps_seen = []
+            for rr in range(o_now):
+                steps_seen.append((rr, (rr + 1) % o_now))
+            w1 = lax.ppermute(w1, axis_key, steps_seen)
+            current_arr = lax.dynamic_update_slice_in_dim(
+                current_arr, w1, (part_now - ix) % o_now * finding, axis=ndim_at
+            )
+            if 2 * ix < o_now:
+                copies = []
+                for rr in range(o_now):
+                    copies.append((rr, (rr - 1) % o_now))
+                response = lax.ppermute(response, axis_key, copies)
+                current_arr = lax.dynamic_update_slice_in_dim(
+                    current_arr, response, (part_now + ix) % o_now * finding, axis=ndim_at
+                )
+        return current_arr
+
+    self_full = sides_process(self_params, "fsdp", 0)
     self_parts = split_flat(self_full, self_layout())
     w_q, w_k, w_v, w_o, b_q, b_v, b_o, gain_one, shift_one = self_parts
     positions = jnp.arange(seq)

time: 2630 us -> 2780 us (1.057)
  local copies, waits for them, and re-layouts: 767 us -> 882 us
  starting transfers between devices: 0.16 us -> 33.9 us
    dynamic_update_slice x0 -> x16, local copies, waits for them, and re-layouts: none -> 93.8 us  [the longest x8 46.9 us: sides_process(): lax.dynamic_update_slice_in_dim(current_arr, w1, (part_now - ix) % o_now...]
    all_gather x1, waiting for transfers between devices: 60.6 us -> 0.01 us  [per_device(): lax.all_gather(self_params, 'fsdp', axis=0, tiled=True)]
    ppermute x0 -> x15, waiting for transfers between devices: none -> 49 us  [the longest x7 37.1 us: sides_process(): response = lax.ppermute(response, axis_key, copies)]
    ppermute x0 -> x15, starting transfers between devices: none -> 33.7 us  [the longest x7 32.6 us: sides_process(): response = lax.ppermute(response, axis_key, copies)]
    unnamed x312 -> x304, local copies, waits for them, and re-layouts: 337 us -> 333 us
    slice x7 -> x8, local copies, waits for them, and re-layouts: 52.2 us -> 56 us  [split_flat(): pieces.append(flat_vec[offset:offset + amount].reshape(layout))]
  transfers between devices with their start and end apart: 4 -> 19, of which waited for: 2 -> 11; matrix products, arithmetic and copies ran while one was open for 14% -> 17% of each run, Pallas kernels for 0% -> 0%
where the time goes in v1:
time: 2780 us; the launch traced here: 2750 us
  blocking collectives  988 us (36%)
  local copies, waits for them, and re-layouts  882 us (32%)
  other arithmetic  680 us (24%)
  matrix products  96.7 us (3%)
  waiting for transfers between devices  55.2 us (2%)
  starting transfers between devices  33.9 us (1%)
    unnamed x1, blocking collectives  964 us
    all_gather x1, other arithmetic, per_device(): ffn_full = lax.all_gather(ffn_params, 'fsdp', axis=0, tiled=True)  401 us
    unnamed x304, local copies, waits for them, and re-layouts  333 us
    all_gather x1, other arithmetic, per_device(): cross_full = lax.all_gather(cross_params, 'fsdp', axis=0, tiled=True)  142 us
    reshape x6, local copies, waits for them, and re-layouts, regroup(): return flat_vec.reshape(groups, replicas, -1).transpose(1, 0, 2).reshape(-1)  133 us
    all_gather x1, other arithmetic, per_device(): lax.all_gather(self_params, 'fsdp', axis=0, tiled=True)  77.7 us
    slice x8, local copies, waits for them, and re-layouts, split_flat(): pieces.append(flat_vec[offset:offset + amount].reshape(layout))  56 us
  transfers between devices with their start and end apart: 19, of which 11 were waited for; matrix products, arithmetic and copies ran while one was open for 17% of the time, Pallas kernels for 0%

profile of v1, /device:TPU:0, one launch (start us, length us, event | category | flops | bytes accessed | tf_op | source)
XLA Modules:
  0.0 2751.9 jit_solution(10041021026785746451)
XLA Ops:
  54.0 14.2 reshape.511
  72.9 10.6 collective-permute-done.7
  245.1 77.7 %reduce.13 = bf16[16,147712]{1,0:T(8,128)(2,1)} reduce(bf16[16,1,147712]{2,1,0:T(2,128)(2,1)} %all-gather.15.cloned.1.call-done, bf16[]{:T(256)} %constant.189), dimensions={1}, to_apply=%all-gather.2.reduce_sub_computation | reduce | bytes 9453570 | tf_op jit(solution)/shard_map/all_gather | solution.py:286
  322.9 10.2 reshape.514
  348.9 141.7 %reduce.11 = bf16[16,209152]{1,0:T(8,128)(2,1)} reduce(bf16[16,1,209152]{2,1,0:T(2,128)(2,1)} %all-gather.11.cloned.1.call-done, bf16[]{:T(256)} %constant.189), dimensions={1}, to_apply=%all-gather.reduce_sub_computation | reduce | bytes 13385730 | tf_op jit(solution)/shard_map/all_gather | solution.py:212
  490.6 13.7 reshape.510
  559.4 400.6 %reduce.12 = bf16[16,590592]{1,0:T(8,128)(2,1)} reduce(bf16[16,1,590592]{2,1,0:T(2,128)(2,1)} %all-gather.13.cloned.1.call-done, bf16[]{:T(256)} %constant.189), dimensions={1}, to_apply=%all-gather.1.reduce_sub_computation | reduce | bytes 37797888 | tf_op jit(solution)/shard_map/all_gather | solution.py:228
  960.0 43.1 %reshape.512 = bf16[9449472]{0:T(1024)(128)(2,1)} reshape(bf16[16,590592]{1,0:T(8,128)(2,1)} %reduce.12) | data formatting | bytes 37797888
  1003.1 14.0 fusion.72
  1188.5 10.3 reshape.495
  1292.6 13.4 reshape.501
  1306.0 10.5 copy.147
  1316.5 10.0 reshape.502
  1336.2 10.8 reshape.504
  1354.1 10.7 reshape.506
  1377.7 80.5 %dynamic-update-slice.6 = f32[9447936]{0:T(1024)} dynamic-update-slice(f32[9447936]{0:T(1024)} %constant_dynamic-update-slice_fusion.25, f32[2359296]{0:T(1024)} %bitcast.182, s32[]{} %constant.201) | dynamic-update-slice | bytes 18874372
  1459.5 80.5 %dynamic-update-slice.8 = f32[9447936]{0:T(1024)} dynamic-update-slice(f32[9447936]{0:T(1024)} %constant_dynamic-update-slice_fusion.24, f32[2359296]{0:T(1024)} %reshape.506, s32[]{} %constant.203) | dynamic-update-slice | bytes 18874372
  1543.9 27.1 pad.14
  1570.9 59.6 %reshape.507 = f32[16,2,295296]{2,1,0:T(2,128)} reshape(f32[9449472]{0:T(1024)} %pad.14) | data formatting | bytes 75595776 | tf_op jit(solution)/shard_map/reshape | solution.py:48
  1630.5 29.9 %copy.148 = f32[2,16,295296]{2,1,0:T(8,128)} copy(f32[2,16,295296]{2,0,1:T(2,128)} %bitcast.175) | data formatting | bytes 75595776 | tf_op jit(solution)/shard_map/transpose | solution.py:48
  1660.4 31.6 %reshape.508 = f32[9449472]{0:T(1024)} reshape(f32[2,16,295296]{2,1,0:T(8,128)} %copy.148) | data formatting | bytes 75595776 | tf_op jit(solution)/shard_map/reshape | solution.py:48
  1692.0 963.5 %all-reduce.8 = (bf16[2363392]{0:T(1024)(128)(2,1)}, bf16[3346432]{0:T(1024)(128)(2,1)}, bf16[9449472]{0:T(1024)(128)(2,1)}) all-reduce(f32[2363392]{0:T(1024)} %reshape.496, f32[3346432]{0:T(1024)} %reshape.502, f32[9449472]{0:T(1024)} %reshape.508), channel_id=2, replica_groups=mesh['dp'=2,'fsdp'=16] {'dp','fsdp'}, use_global_device_ids=true, to_apply=%region_28.29.clone | all-reduce | flops 15159296 | bytes 90955776
  2678.3 15.3 all-gather.4
  2714.9 26.9 convert_reduce_fusion
  (542 shorter events, 629.8 us)
Async XLA Ops:
  7.2 237.9 %all-gather.15.cloned.1.call-start = ((), (), s32[]{:S(2)}) async-start(), calls=%async_computation.2 | async-start | bytes 10044416 | tf_op jit(solution)/shard_map/all_gather | solution.py:286
  11.7 337.2 %all-gather.11.cloned.1.call-start = ((), (), s32[]{:S(2)}) async-start(), calls=%async_computation | async-start | bytes 14222336 | tf_op jit(solution)/shard_map/all_gather | solution.py:212
  17.4 98.9 %copy-start.50 = (bf16[2,257,1408]{2,0,1:T(2,128)(2,1)S(1)}, bf16[2,257,1408]{2,0,1:T(2,128)(2,1)}, u32[]{:S(2)}) copy-start(bf16[2,257,1408]{2,0,1:T(2,128)(2,1)} %param.9) | copy-start | bytes 4342276
  17.4 542.0 %all-gather.13.cloned.1.call-start = ((), (), s32[]{:S(2)}) async-start(), calls=%async_computation.1 | async-start | bytes 40160256 | tf_op jit(solution)/shard_map/all_gather | solution.py:228
  17.5 10.3 collective-permute-start
  18.0 15.7 collective-permute-start.1
  27.8 15.2 collective-permute-start.2
  33.6 82.7 %copy-start.70 = (bf16[147712]{0:T(1024)(128)(2,1)}, bf16[147712]{0:T(1024)(128)(2,1)S(1)}, u32[]{:S(2)}) copy-start(bf16[147712]{0:T(1024)(128)(2,1)S(1)} %collective-permute-done.1) | copy-start | bytes 886276
  33.6 15.1 collective-permute-start.3
  43.0 10.9 collective-permute-start.4
  48.7 19.5 collective-permute-start.5
  54.0 18.8 collective-permute-start.6
  68.2 2646.7 %all-gather.17.cloned.1.call-start = ((), (), s32[]{:S(2)}) async-start(), calls=%async_computation.3 | async-start | bytes 3543552 | tf_op jit(solution)/shard_map/all_gather | solution.py:337
  68.2 15.3 collective-permute-start.7
  72.7 15.5 collective-permute-start.8
  83.5 11.9 collective-permute-start.9
  88.2 11.9 collective-permute-start.10
  95.4 13.3 collective-permute-start.11
  100.1 14.9 collective-permute-start.12
  108.7 94.6 %collective-permute-start.13 = (bf16[147712]{0:T(1024)(128)(2,1)}, bf16[147712]{0:T(1024)(128)(2,1)}, u32[]{:S(2)}, u32[]{:S(2)}) collective-permute-start(bf16[147712]{0:T(1024)(128)(2,1)} %collective-permute-done.11), channel_id=1, source_target_pairs={{0,15},{1,0},{2,1},{3,2},{4,3},{5,4},{6,5},{7,6},{8,7},{9,8},{10,9... | collective-permute-start | bytes 886280 | tf_op jit(solution)/shard_map/ppermute | solution.py:183
  115.0 94.2 %collective-permute-start.14 = (bf16[147712]{0:T(1024)(128)(2,1)}, bf16[147712]{0:T(1024)(128)(2,1)}, u32[]{:S(2)}, u32[]{:S(2)}) collective-permute-start(bf16[147712]{0:T(1024)(128)(2,1)} %collective-permute-done.12), channel_id=1, source_target_pairs={{0,1},{1,2},{2,3},{3,4},{4,5},{5,6},{6,7},{7,8},{8,9},{9,10},{10,1... | collective-permute-start | bytes 886280 | tf_op jit(solution)/shard_map/ppermute | solution.py:175
  239.2 83.7 %copy-start.30 = (bf16[128,768]{0,1:T(8,128)(2,1)}, bf16[128,768]{0,1:T(8,128)(2,1)S(1)}, u32[]{:S(2)}) copy-start(bf16[128,768]{0,1:T(8,128)(2,1)S(1)} %convert_element_type.316) | copy-start | bytes 589828
  1459.5 81.8 %copy-start.104 = (f32[768]{0:T(1024)S(1)}, f32[768]{0:T(1024)}, u32[]{:S(2)}) copy-start(f32[768]{0:T(1024)} %get-tuple-element.7) | copy-start | bytes 9220
  1459.5 83.1 %copy-start.100 = (f32[768]{0:T(1024)S(1)}, f32[768]{0:T(1024)}, u32[]{:S(2)}) copy-start(f32[768]{0:T(1024)} %get-tuple-element.13) | copy-start | bytes 9220
  (126 other events, 1407.2 us)
Sparse Core Ops, SparseCore 0:
  11.8 106.7 all-gather.14
  121.5 107.5 all-gather.10
  231.3 186.1 all-gather.12
  2678.4 36.3 all-gather.16
